TPU v7x, 32 devices: a whole 2x2x4 slice. The times are simulated.
32 devices in a mesh: groups: 2 (over x), gx: 16 (over z, y, core).
Axes of the slice: x: 2, y: 2, z: 4, core: 2. Of those that a mesh axis runs over, the one named last changes fastest.
Arguments:
- activations: bfloat16 [1024, 18432], P('groups', 'gx'), parts along dimension 0, may hold values from -25 to 25, as said below
- norm_gain: float32 [18432], P('gx'), may hold values from 0.1 to 1.9
- w_up: bfloat16 [18432, 8192], P('gx'), may hold values from -0.0625 to 0.0625
- w_down: bfloat16 [8192, 18432], P(None, 'gx'), may hold values from -0.0625 to 0.0625
Outputs:
- layer_out: bfloat16 [1024, 18432], P('groups', 'gx'), parts along dimension 0
There are 2 independent parts, one for each index of `groups`. A program takes and returns all parts, laid end to end along the dimension named above; an argument that names none is the same for every part. Nothing has to cross between parts.
Inputs may be any that keep to these rules, and one draw needn't show every extreme that they name: Every batch row of activations has a root-mean-square over the features of at least 0.1.
All inputs are finite; a program needn't handle non-finite values.
Results may differ from a plain program's by a relative error of at most 0.0043.
Values may be sent and summed in bfloat16 or wider, within the bound.
A program may use at most 128 MiB of HBM per device.

v0:
```python
import jax
import jax.numpy as jnp
from jax import lax
from jax.sharding import PartitionSpec as P

D = 18432


def local(activations, norm_gain, w_up, w_down):
    wide_act = activations.astype(jnp.float32)
    squares = lax.psum(jnp.sum(wide_act * wide_act, axis=1), "gx")
    row_scale = lax.rsqrt(squares / D + 1e-06)
    normed = (wide_act * norm_gain[None, :]).astype(jnp.bfloat16)
    shares = lax.psum_scatter(
        lax.dot_general(w_up, normed, (((0,), (1,)), ((), ())), preferred_element_type=jnp.float32),
        "gx",
        scatter_dimension=0,
        tiled=True,
    )
    hidden = jax.nn.gelu(shares * row_scale[None, :], approximate=False).astype(jnp.bfloat16)
    local_out = lax.dot_general(
        lax.all_gather(hidden, "gx", axis=0, tiled=True),
        w_down,
        (((0,), (0,)), ((), ())),
        preferred_element_type=jnp.float32,
    )
    return (wide_act + local_out).astype(jnp.bfloat16)


def solution(mesh):
    return jax.shard_map(
        local,
        mesh=mesh,
        in_specs=(P("groups", "gx"), P("gx"), P("gx", None), P(None, "gx")),
        out_specs=P("groups", "gx"),
        check_vma=False,
    )
```

profile of v0, /device:TPU:0, one launch (start us, length us, event | category | flops | bytes accessed | tf_op | source)
XLA Modules:
  0.0 312.0 jit_solution(17734944829562289535)
XLA Ops:
  6.5 0.0 reduce-scatter.2.cloned.1.call-start
  6.5 18.3 %convolution_bitcast_fusion = f32[8192,512]{0,1:T(8,128)} fusion(bf16[1152,8192]{1,0:T(8,128)(2,1)} %param.6, bf16[512,1152]{1,0:T(8,128)(2,1)} %param.4, f32[1152]{0:T(1024)} %param.5), kind=kOutput, calls=%fused_computation | convolution fusion | flops 9665445888 | bytes 36835840 | tf_op jit(solution)/shard_map/dot_general | solution.py:15
  24.9 0.0 copy-start
  24.9 0.0 reduce-scatter.2.cloned.1.call-update
  24.9 0.0 all-gather.2.cloned.1.call-start
  24.9 1.2 copy-done
  26.1 0.3 fusion.2
  26.4 34.9 %psum.7 = f32[512]{0:T(512)S(1)} all-reduce(f32[512]{0:T(512)S(1)} %fusion.2), channel_id=1, replica_groups=mesh['groups'=2,'gx'=16] {'gx'}, use_global_device_ids=true, to_apply=%region_2.0 | all-reduce | flops 512 | bytes 4096 | tf_op jit(solution)/shard_map/psum | solution.py:11
  61.4 144.9 %reduce-scatter.2.cloned.1.call-done = f32[512,512]{0,1:T(8,128)} async-done(((f32[8192,512]{0,1:T(8,128)}), f32[512,512]{0,1:T(8,128)}) %reduce-scatter.2.cloned.1.call-update) | async-done | bytes 1048592 | tf_op jit(solution)/shard_map/reduce_scatter | solution.py:14
  206.3 4.3 %fusion.7 = bf16[512,512]{0,1:T(8,128)(2,1)} fusion(f32[512,512]{0,1:T(8,128)} %reduce-scatter.2.cloned.1.call-done, f32[512]{0:T(512)S(1)} %add_rsqrt_fusion), kind=kLoop, calls=%fused_computation.11 | loop fusion | flops 17301504 | bytes 1574912 | tf_op jit(solution)/shard_map/convert_element_type | solution.py:20
  210.6 0.0 all-gather.2.cloned.1.call-update
  210.6 77.3 %all-gather.2.cloned.1.call-done = bf16[8192,512]{0,1:T(8,128)(2,1)} async-done(((bf16[512,512]{0,1:T(8,128)(2,1)}), bf16[8192,512]{0,1:T(8,128)(2,1)}) %all-gather.2.cloned.1.call-update) | async-done | bytes 8388624 | tf_op jit(solution)/shard_map/all_gather | solution.py:22
  287.8 17.3 %fusion = bf16[512,1152]{1,0:T(8,128)(2,1)} fusion(bf16[8192,512]{0,1:T(8,128)(2,1)} %all-gather.2.cloned.1.call-done, bf16[8192,1152]{1,0:T(8,128)(2,1)} %param.7, bf16[512,1152]{1,0:T(8,128)(2,1)S(1)} %copy-done), kind=kOutput, calls=%fused_computation.4 | convolution fusion | flops 9665445888 | bytes 29622272 | tf_op jit(solution)/shard_map/dot_general | solution.py:21
  (1 shorter events, 0.0 us)
Async XLA Ops:
  6.5 199.8 %reduce-scatter.2.cloned.1.call-start = ((), (), s32[]{:S(2)}) async-start(), calls=%async_computation.1 | async-start | bytes 17825792 | tf_op jit(solution)/shard_map/reduce_scatter | solution.py:14
  24.9 1.3 copy-start
  24.9 262.9 %all-gather.2.cloned.1.call-start = ((), (), s32[]{:S(2)}) async-start(), calls=%async_computation.2 | async-start | bytes 8912896 | tf_op jit(solution)/shard_map/all_gather | solution.py:22
Sparse Core Ops, SparseCore 0:
  25.0 181.2 reduce-scatter.1
  210.7 77.0 all-gather.1
where the time goes:
time: 312 us
  waiting for transfers between devices  222 us (71%)
  matrix products  35.6 us (11%)
  blocking collectives  34.9 us (11%)
  between operations  13.4 us (4%)
  other arithmetic  4.58 us (1%)
    reduce_scatter x1, waiting for transfers between devices, local(): lax.psum_scatter(lax.dot_general(w_up, normed, (((0,), (1,)), ((), ())),...  145 us
    all_gather x1, waiting for transfers between devices, local(): lax.all_gather(hidden, 'gx', axis=0, tiled=True)  77.3 us
    psum x1, blocking collectives, local(): squares = lax.psum(jnp.sum(wide_act * wide_act, axis=1), 'gx')  34.9 us
    dot_general x1, matrix products, local(): lax.dot_general(w_up, normed, (((0,), (1,)), ((), ())), preferred_element...  18.3 us
    dot_general x1, matrix products, local(): lax.dot_general(lax.all_gather(hidden, 'gx', axis=0, tiled=True), w_down,...  17.3 us
  transfers between devices with their start and end apart: 2, of which 2 were waited for; matrix products, arithmetic and copies ran while one was open for 0% of the time, Pallas kernels for 0%

commit v1 on v0

v1 whole, which is shorter than its diff:
```python
import functools

import jax
import jax.numpy as jnp
from jax import lax
from jax.experimental import pallas as pl
from jax.experimental.pallas import tpu as pltpu
from jax.sharding import PartitionSpec as P

CHUNK = 1024
MESH = pl.DeviceIdType.MESH


def kernel(dims, act, gain, wup, wdn, out, *scratch):
    n, depth, width, chunks = dims
    (normed, acc, scale, wub, wdb, keep0, keep1, keep2, s_core, r_core, s_y, r_y, s_z, r_z, gath, sq_s, sq_r, sq_z,
     wu_sem, wd_sem, cs, cr, ys, yr, zs, zr, ags, agr, ays, ayr, acs, acr, qs, qr, qzs, qzr) = scratch
    batch = act.shape[0]
    half = CHUNK // 2
    rows = batch // 2
    nz = n // 4
    block = rows // nz

    me = lax.axis_index("gx")
    core = lax.rem(me, 2)
    y = lax.rem(me // 2, 2)
    z = me // 4
    core_peer = me + 1 - 2 * core
    y_peer = me + 2 - 4 * y
    z_others = [lax.rem(z + j, nz) for j in range(1, nz)]

    def z_peer(other):
        return other * 4 + y * 2 + core

    def rdma(src, dst, send, recv, peer):
        return pltpu.make_async_remote_copy(
            src_ref=src, dst_ref=dst, send_sem=send, recv_sem=recv, device_id={"gx": peer}, device_id_type=MESH
        )

    def up_copies(c, slot):
        return [
            pltpu.make_async_copy(
                wup.at[:, pl.ds(pl.multiple_of(c * CHUNK + which * half, half), half)], wub.at[slot, k], wu_sem.at[slot, k]
            )
            for k, which in enumerate((1 - core, core))
        ]

    def down_copy(c, slot):
        return pltpu.make_async_copy(
            wdn.at[pl.ds(pl.multiple_of(c * CHUNK, CHUNK), CHUNK), :], wdb.at[slot], wd_sem.at[slot]
        )

    def core_rs(c):
        return rdma(s_core.at[c], r_core.at[c], cs.at[c], cr.at[c], core_peer)

    def y_rs(c):
        return rdma(s_y.at[c], r_y.at[c], ys.at[c], yr.at[c], y_peer)

    def z_rs_to(c, o):
        return rdma(
            s_z.at[c, pl.ds(pl.multiple_of(o * block, block), block)], r_z.at[c, z], zs.at[c, o], zr.at[c, z], z_peer(o)
        )

    def z_rs_from(c, o):
        return rdma(
            s_z.at[c, pl.ds(pl.multiple_of(o * block, block), block)], r_z.at[c, o], zs.at[c, o], zr.at[c, o], z_peer(o)
        )

    def z_rows(o):
        return pl.ds(pl.multiple_of(y * rows + o * block, block), block)

    def z_ag_to(c, o):
        part = gath.at[c, core, z_rows(z)]
        return rdma(part, part, ags.at[c, o], agr.at[c, z], z_peer(o))

    def z_ag_from(c, o):
        part = gath.at[c, core, z_rows(o)]
        return rdma(part, part, ags.at[c, o], agr.at[c, o], z_peer(o))

    def y_part(c, which):
        part = gath.at[c, core, pl.ds(pl.multiple_of(which * rows, rows), rows)]
        return rdma(part, part, ays.at[c], ayr.at[c], y_peer)

    def core_part(c, which):
        part = gath.at[c, which]
        return rdma(part, part, acs.at[c], acr.at[c], core_peer)

    def sq_core():
        return rdma(sq_s.at[0], sq_r.at[0], qs.at[0], qr.at[0], core_peer)

    def sq_y():
        return rdma(sq_s.at[1], sq_r.at[1], qs.at[1], qr.at[1], y_peer)

    def sq_to(o):
        return rdma(sq_s.at[2], sq_z.at[z], qzs.at[o], qzr.at[z], z_peer(o))

    def sq_from(o):
        return rdma(sq_s.at[2], sq_z.at[o], qzs.at[o], qzr.at[o], z_peer(o))

    for slot in range(2):
        for copy in up_copies(slot, slot):
            copy.start()
        down_copy(slot, slot).start()

    barrier = pltpu.get_barrier_semaphore()
    peers = [core_peer, y_peer] + [z_peer(o) for o in z_others]
    for peer in peers:
        pl.semaphore_signal(barrier, inc=1, device_id={"gx": peer}, device_id_type=MESH)

    wide = act[...].astype(jnp.float32)
    normed[...] = (wide * gain[...]).astype(jnp.bfloat16)
    acc[...] = wide
    squares = jnp.broadcast_to(jnp.sum(wide * wide, axis=1, keepdims=True), (batch, 128))
    sq_s[0] = squares.T[:8]

    pl.semaphore_wait(barrier, len(peers))
    sq_core().start()

    def up(c):
        slot = lax.rem(c, 2)
        for copy in up_copies(c, slot):
            copy.wait()
        s_core[c] = jnp.dot(normed[...], wub[slot, 0], preferred_element_type=jnp.float32).astype(jnp.bfloat16)
        core_rs(c).start()
        keep0[slot] = jnp.dot(normed[...], wub[slot, 1], preferred_element_type=jnp.float32)

        @pl.when(c + 2 < chunks)
        def _():
            for copy in up_copies(c + 2, slot):
                copy.start()

    def sum_core(c):
        slot = lax.rem(c, 2)
        core_rs(c).wait_recv()
        theirs = pl.ds(pl.multiple_of((1 - y) * rows, rows), rows)
        mine = pl.ds(pl.multiple_of(y * rows, rows), rows)
        s_y[c] = (keep0[slot, theirs] + r_core[c, theirs].astype(jnp.float32)).astype(jnp.bfloat16)
        y_rs(c).start()
        keep1[slot] = keep0[slot, mine] + r_core[c, mine].astype(jnp.float32)

    def sum_y(c):
        slot = lax.rem(c, 2)
        y_rs(c).wait_recv()
        s_z[c] = (keep1[slot] + r_y[c].astype(jnp.float32)).astype(jnp.bfloat16)
        for o in z_others:
            z_rs_to(c, o).start()
        mine = pl.ds(pl.multiple_of(z * block, block), block)
        keep2[slot] = keep1[slot, mine] + r_y[c, mine].astype(jnp.float32)

    def sum_z(c):
        slot = lax.rem(c, 2)
        total = keep2[slot]
        for o in z_others:
            z_rs_from(c, o).wait_recv()
            total = total + r_z[c, o].astype(jnp.float32)
        pre = total * scale[z_rows(z), :][:, :1]
        hidden = 0.5 * pre * (1.0 + lax.erf(pre * 0.7071067811865476))
        gath[c, core, z_rows(z)] = hidden.astype(jnp.bfloat16)
        for o in z_others:
            z_ag_to(c, o).start()

    def gather_z(c):
        for o in z_others:
            z_ag_from(c, o).wait_recv()
        y_part(c, y).start()

    def gather_y(c):
        y_part(c, 1 - y).wait_recv()
        core_part(c, core).start()

    def down(c):
        slot = lax.rem(c, 2)
        down_copy(c, slot).wait()
        core_part(c, 1 - core).wait_recv()
        acc[...] += jnp.dot(gath[c, 0], wdb[slot, :half], preferred_element_type=jnp.float32)
        acc[...] += jnp.dot(gath[c, 1], wdb[slot, half:], preferred_element_type=jnp.float32)

        @pl.when(c + 2 < chunks)
        def _():
            down_copy(c + 2, slot).start()

    stages = [(5, gather_y), (4, gather_z), (3, sum_z), (2, sum_y), (1, sum_core), (0, up), (6, down)]

    def step(t, carry):
        @pl.when(t == 1)
        def _():
            sq_core().wait_recv()
            sq_s[1] = sq_s[0] + sq_r[0]
            sq_y().start()

        @pl.when(t == 2)
        def _():
            sq_y().wait_recv()
            sq_s[2] = sq_s[1] + sq_r[1]
            for o in z_others:
                sq_to(o).start()

        @pl.when(t == 3)
        def _():
            total = sq_s[2]
            for o in z_others:
                sq_from(o).wait_recv()
                total = total + sq_z[o]
            row_scale = lax.rsqrt(total / (depth * n) + 1e-06)
            scale[...] = jnp.broadcast_to(row_scale[:1], (128, batch)).T

        for offset, stage in stages:
            c = t - offset

            @pl.when(jnp.logical_and(c >= 0, c < chunks))
            def _(c=c, stage=stage):
                stage(c)

        return carry

    lax.fori_loop(0, chunks + 6, step, 0)

    out[...] = acc[...].astype(jnp.bfloat16)

    sq_core().wait_send()
    sq_y().wait_send()
    for o in z_others:
        sq_to(o).wait_send()

    def drain(c, carry):
        core_rs(c).wait_send()
        y_rs(c).wait_send()
        for o in z_others:
            z_rs_to(c, o).wait_send()
            z_ag_to(c, o).wait_send()
        y_part(c, y).wait_send()
        core_part(c, core).wait_send()
        return carry

    lax.fori_loop(0, chunks, drain, 0)


def local(n, activations, norm_gain, w_up, w_down):
    batch, depth = activations.shape
    width = w_up.shape[1]
    chunks = width // CHUNK
    half, rows, nz = CHUNK // 2, batch // 2, n // 4
    block = rows // nz
    bf16, f32 = jnp.bfloat16, jnp.float32
    vmem, dma = pltpu.VMEM, pltpu.SemaphoreType.DMA
    in_vmem = pl.BlockSpec(memory_space=pltpu.VMEM)
    in_hbm = pl.BlockSpec(memory_space=pl.ANY)
    return pl.pallas_call(
        functools.partial(kernel, (n, depth, width, chunks)),
        out_shape=jax.ShapeDtypeStruct((batch, depth), bf16),
        in_specs=[in_vmem, in_vmem, in_hbm, in_hbm],
        out_specs=in_vmem,
        scratch_shapes=[
            vmem((batch, depth), bf16),
            vmem((batch, depth), f32),
            vmem((batch, 128), f32),
            vmem((2, 2, depth, half), bf16),
            vmem((2, CHUNK, depth), bf16),
            vmem((2, batch, half), f32),
            vmem((2, rows, half), f32),
            vmem((2, block, half), f32),
            vmem((chunks, batch, half), bf16),
            vmem((chunks, batch, half), bf16),
            vmem((chunks, rows, half), bf16),
            vmem((chunks, rows, half), bf16),
            vmem((chunks, rows, half), bf16),
            vmem((chunks, nz, block, half), bf16),
            vmem((chunks, 2, batch, half), bf16),
            vmem((3, 8, batch), f32),
            vmem((2, 8, batch), f32),
            vmem((nz, 8, batch), f32),
            dma((2, 2)),
            dma((2,)),
            dma((chunks,)),
            dma((chunks,)),
            dma((chunks,)),
            dma((chunks,)),
            dma((chunks, nz)),
            dma((chunks, nz)),
            dma((chunks, nz)),
            dma((chunks, nz)),
            dma((chunks,)),
            dma((chunks,)),
            dma((chunks,)),
            dma((chunks,)),
            dma((2,)),
            dma((2,)),
            dma((nz,)),
            dma((nz,)),
        ],
        compiler_params=pltpu.CompilerParams(
            collective_id=0, has_side_effects=True, vmem_limit_bytes=60 * 1024 * 1024
        ),
        cost_estimate=pl.CostEstimate(
            flops=4 * batch * depth * width, bytes_accessed=4 * depth * width, transcendentals=batch * width // n
        ),
    )(activations, norm_gain[None, :], w_up, w_down)


def solution(mesh):
    return jax.shard_map(
        functools.partial(local, mesh.shape["gx"]),
        mesh=mesh,
        in_specs=(P("groups", "gx"), P("gx"), P("gx", None), P(None, "gx")),
        out_specs=P("groups", "gx"),
        check_vma=False,
    )
```

time: 312 us -> 130 us (0.42)
  waiting for transfers between devices: 222 us -> 0 us
  Pallas kernels: 0 us -> 126 us
  matrix products: 35.6 us -> 0 us
  blocking collectives: 34.9 us -> 0 us
  between operations: 13.4 us -> 0.01 us
  other arithmetic: 4.58 us -> 0 us
    reduce_scatter x1 -> x0, waiting for transfers between devices: 145 us -> none  [local(): lax.psum_scatter(lax.dot_general(w_up, normed, (((0,), (1,)), ((), ())),...]
    pallas_call x0 -> x1, Pallas kernels: none -> 126 us  [local(): pl.pallas_call(functools.partial(kernel, (n, depth, width, chunks)), out_...]
    all_gather x1 -> x0, waiting for transfers between devices: 77.3 us -> none  [local(): lax.all_gather(hidden, 'gx', axis=0, tiled=True)]
    dot_general x2 -> x0, matrix products: 35.6 us -> none  [the longest x1 18.3 us: local(): lax.dot_general(w_up, normed, (((0,), (1,)), ((), ())), preferred_element...]
    psum x1 -> x0, blocking collectives: 34.9 us -> none  [local(): squares = lax.psum(jnp.sum(wide_act * wide_act, axis=1), 'gx')]
    convert_element_type x1 -> x0, other arithmetic: 4.27 us -> none  [local(): jax.nn.gelu(shares * row_scale[None, :], approximate=False)]
  transfers between devices with their start and end apart: 2 -> 0, of which waited for: 2 -> 0; matrix products, arithmetic and copies ran while one was open for 0% -> 0% of each run, Pallas kernels for 0% -> 0%
where the time goes in v1:
time: 130 us
  Pallas kernels  126 us (97%)
  local copies, waits for them, and re-layouts  3.67 us (3%)
    pallas_call x1, Pallas kernels, local(): pl.pallas_call(functools.partial(kernel, (n, depth, width, chunks)), out_...  126 us

profile of v1, /device:TPU:0, one launch (start us, length us, event | category | flops | bytes accessed | tf_op | source)
XLA Modules:
  0.0 130.0 jit_solution(3560367731338406627)
XLA Ops:
  0.0 1.3 broadcast_in_dim.3.gain
  1.3 126.3 %shard_map.46 = bf16[512,1152]{1,0:T(8,128)(2,1)} custom-call(bf16[512,1152]{1,0:T(8,128)(2,1)} %act.1, f32[1,1152]{1,0:T(1,128)} %broadcast_in_dim.3.gain, bf16[1152,8192]{1,0:T(8,128)(2,1)} %wup.1, bf16[8192,1152]{1,0:T(8,128)(2,1)} %wdn.1), custom_call_target="tpu_custom_call" | custom-call | flops 19327352832 | bytes 37748736 | tf_op jit(solution)/shard_map/pallas_call | solution.py:248
  127.6 2.4 %copy.6 = bf16[512,1152]{1,0:T(8,128)(2,1)} copy(bf16[512,1152]{1,0:T(8,128)(2,1)} %shard_map.46) | data formatting | bytes 2359296

commit v2 on v1

--- a/solution.py
+++ b/solution.py
@@ -7,19 +7,19 @@
 from jax.experimental.pallas import tpu as pltpu
 from jax.sharding import PartitionSpec as P
 
-CHUNK = 1024
+CHUNK = 512
+EVERY = 4
+LAST = 14
 MESH = pl.DeviceIdType.MESH
 
 
 def kernel(dims, act, gain, wup, wdn, out, *scratch):
     n, depth, width, chunks = dims
-    (normed, acc, scale, wub, wdb, keep0, keep1, keep2, s_core, r_core, s_y, r_y, s_z, r_z, gath, sq_s, sq_r, sq_z,
+    (normed, acc, scale, wub, wdb, keep, s_core, r_core, s_y, r_y, s_z, r_z, s_m, r_m, gath, sq_s, sq_r, sq_z,
      wu_sem, wd_sem, cs, cr, ys, yr, zs, zr, ags, agr, ays, ayr, acs, acr, qs, qr, qzs, qzr) = scratch
     batch = act.shape[0]
     half = CHUNK // 2
-    rows = batch // 2
     nz = n // 4
-    block = rows // nz
 
     me = lax.axis_index("gx")
     core = lax.rem(me, 2)
@@ -32,6 +32,13 @@
     def z_peer(other):
         return other * 4 + y * 2 + core
 
+    tree = nz == 4
+    pair = z // 2
+    near = z + 1 - 2 * lax.rem(z, 2)
+    far = (2 - pair, 3 - 3 * pair)
+    at_end = jnp.logical_or(z == 0, z == nz - 1)
+    in_middle = jnp.logical_not(at_end)
+
     def rdma(src, dst, send, recv, peer):
         return pltpu.make_async_remote_copy(
             src_ref=src, dst_ref=dst, send_sem=send, recv_sem=recv, device_id={"gx": peer}, device_id_type=MESH
@@ -53,32 +60,62 @@
     def core_rs(c):
         return rdma(s_core.at[c], r_core.at[c], cs.at[c], cr.at[c], core_peer)
 
-    def y_rs(c):
-        return rdma(s_y.at[c], r_y.at[c], ys.at[c], yr.at[c], y_peer)
-
-    def z_rs_to(c, o):
+    def area(start, size):
+        return pl.ds(pl.multiple_of(start, 16), size)
+
+    def shape_of(z_first):
+        if z_first:
+            z_len = batch // nz
+            return 0, z_len, z * z_len, z_len // 2
+        y_len = batch // 2
+        return y * y_len, y_len // nz, 0, y_len
+
+    def y_rs(zf, c):
+        y_len = shape_of(zf)[3]
+        return rdma(s_y.at[c, pl.ds(0, y_len)], r_y.at[c, pl.ds(0, y_len)], ys.at[c], yr.at[c], y_peer)
+
+    def z_end(zf, c):
+        z_len = shape_of(zf)[1]
+        three = area((1 - pair) * z_len, 3 * z_len)
+        return rdma(s_z.at[c, three], r_z.at[c, three], zs.at[c, 0], zr.at[c, 0], z_peer(near))
+
+    def z_mid(zf, c):
+        z_len = shape_of(zf)[1]
         return rdma(
-            s_z.at[c, pl.ds(pl.multiple_of(o * block, block), block)], r_z.at[c, z], zs.at[c, o], zr.at[c, z], z_peer(o)
+            s_z.at[c, area(near * z_len, z_len)], r_m.at[c, 0, pl.ds(0, z_len)], zs.at[c, 0], zr.at[c, 0], z_peer(near)
         )
 
-    def z_rs_from(c, o):
+    def z_merged(zf, c, j):
+        z_len = shape_of(zf)[1]
         return rdma(
-            s_z.at[c, pl.ds(pl.multiple_of(o * block, block), block)], r_z.at[c, o], zs.at[c, o], zr.at[c, o], z_peer(o)
+            s_m.at[c, j, pl.ds(0, z_len)], r_m.at[c, 1, pl.ds(0, z_len)], zs.at[c, 1 + j], zr.at[c, 1], z_peer(far[j])
         )
 
-    def z_rows(o):
-        return pl.ds(pl.multiple_of(y * rows + o * block, block), block)
-
-    def z_ag_to(c, o):
-        part = gath.at[c, core, z_rows(z)]
-        return rdma(part, part, ags.at[c, o], agr.at[c, z], z_peer(o))
-
-    def z_ag_from(c, o):
-        part = gath.at[c, core, z_rows(o)]
-        return rdma(part, part, ags.at[c, o], agr.at[c, o], z_peer(o))
-
-    def y_part(c, which):
-        part = gath.at[c, core, pl.ds(pl.multiple_of(which * rows, rows), rows)]
+    def z_direct(zf, c, o, slot):
+        z_len = shape_of(zf)[1]
+        return rdma(s_z.at[c, area(o * z_len, z_len)], r_z.at[c, area(slot * z_len, z_len)], zs.at[c, o], zr.at[c, slot], z_peer(o))
+
+    def z_part(zf, c, o):
+        base, z_len = shape_of(zf)[:2]
+        return gath.at[c, core, area(base + o * z_len, z_len)]
+
+    def g_near(zf, c, o):
+        return rdma(z_part(zf, c, o), z_part(zf, c, o), ags.at[c, 0], agr.at[c, 0], z_peer(near))
+
+    def g_far(zf, c, o, slot):
+        return rdma(z_part(zf, c, o), z_part(zf, c, o), ags.at[c, 1], agr.at[c, slot], z_peer(far[0]))
+
+    def g_two(zf, c):
+        base, z_len = shape_of(zf)[:2]
+        part = gath.at[c, core, area(base + (1 - pair) * 2 * z_len, 2 * z_len)]
+        return rdma(part, part, ags.at[c, 2], agr.at[c, 1], z_peer(near))
+
+    def g_direct(zf, c, o, slot):
+        return rdma(z_part(zf, c, slot), z_part(zf, c, slot), ags.at[c, o], agr.at[c, slot], z_peer(o))
+
+    def y_part(zf, c, which):
+        base, y_len = shape_of(zf)[2:]
+        part = gath.at[c, core, area(base + which * y_len, y_len)]
         return rdma(part, part, ays.at[c], ayr.at[c], y_peer)
 
     def core_part(c, which):
@@ -122,50 +159,118 @@
             copy.wait()
         s_core[c] = jnp.dot(normed[...], wub[slot, 0], preferred_element_type=jnp.float32).astype(jnp.bfloat16)
         core_rs(c).start()
-        keep0[slot] = jnp.dot(normed[...], wub[slot, 1], preferred_element_type=jnp.float32)
+        keep[c] = jnp.dot(normed[...], wub[slot, 1], preferred_element_type=jnp.float32)
 
         @pl.when(c + 2 < chunks)
         def _():
             for copy in up_copies(c + 2, slot):
                 copy.start()
 
+    def send_y(zf, c):
+        base, y_len = shape_of(zf)[2:]
+        s_y[c, :y_len] = keep[c, area(base + (1 - y) * y_len, y_len)].astype(jnp.bfloat16)
+        y_rs(zf, c).start()
+
+    def take_y(zf, c):
+        base, y_len = shape_of(zf)[2:]
+        y_rs(zf, c).wait_recv()
+        keep[c, area(base + y * y_len, y_len)] += r_y[c, :y_len].astype(jnp.float32)
+
+    def send_z(zf, c):
+        base, z_len = shape_of(zf)[:2]
+        s_z[c, : nz * z_len] = keep[c, area(base, nz * z_len)].astype(jnp.bfloat16)
+        if not tree:
+            for o in z_others:
+                z_direct(zf, c, o, z).start()
+            return
+
+        @pl.when(at_end)
+        def _():
+            z_end(zf, c).start()
+
+        @pl.when(in_middle)
+        def _():
+            z_mid(zf, c).start()
+
+    def merge_z(zf, c):
+        base, z_len = shape_of(zf)[:2]
+        if not tree:
+            return
+
+        @pl.when(in_middle)
+        def _():
+            z_end(zf, c).wait_recv()
+            for j in range(2):
+                mine = keep[c, area(base + far[j] * z_len, z_len)]
+                theirs = r_z[c, area(far[j] * z_len, z_len)].astype(jnp.float32)
+                s_m[c, j, :z_len] = (mine + theirs).astype(jnp.bfloat16)
+                z_merged(zf, c, j).start()
+            keep[c, area(base + z * z_len, z_len)] += r_z[c, area(z * z_len, z_len)].astype(jnp.float32)
+
+    def take_z(zf, c):
+        base, z_len = shape_of(zf)[:2]
+        own = area(base + z * z_len, z_len)
+        if not tree:
+            for o in z_others:
+                z_direct(zf, c, o, o).wait_recv()
+                keep[c, own] += r_z[c, area(o * z_len, z_len)].astype(jnp.float32)
+            return
+
+        @pl.when(at_end)
+        def _():
+            z_mid(zf, c).wait_recv()
+            keep[c, own] += r_m[c, 0, :z_len].astype(jnp.float32)
+
+        z_merged(zf, c, 0).wait_recv()
+        keep[c, own] += r_m[c, 1, :z_len].astype(jnp.float32)
+
+    def activate(zf, c):
+        z_base, z_len, y_base, y_len = shape_of(zf)
+        own = area(y_base + y * y_len, y_len) if zf else area(z_base + z * z_len, z_len)
+        pre = keep[c, own] * scale[own, :][:, :1]
+        hidden = 0.5 * pre * (1.0 + lax.erf(pre * 0.7071067811865476))
+        gath[c, core, own] = hidden.astype(jnp.bfloat16)
+
+    def spread_z(zf, c):
+        if not tree:
+            for o in z_others:
+                g_direct(zf, c, o, z).start()
+            return
+        g_near(zf, c, z).start()
+        g_far(zf, c, z, 1 + at_end.astype(jnp.int32)).start()
+
+    def forward_z(zf, c):
+        if not tree:
+            return
+
+        @pl.when(in_middle)
+        def _():
+            g_far(zf, c, far[0], 1).wait_recv()
+            g_far(zf, c, far[1], 2).wait_recv()
+            g_two(zf, c).start()
+
+    def gathered_z(zf, c):
+        if not tree:
+            for o in z_others:
+                g_direct(zf, c, o, o).wait_recv()
+            return
+        g_near(zf, c, near).wait_recv()
+
+        @pl.when(at_end)
+        def _():
+            g_two(zf, c).wait_recv()
+
+    def spread_y(zf, c):
+        y_part(zf, c, y).start()
+
+    def gathered_y(zf, c):
+        y_part(zf, c, 1 - y).wait_recv()
+
     def sum_core(c):
-        slot = lax.rem(c, 2)
         core_rs(c).wait_recv()
-        theirs = pl.ds(pl.multiple_of((1 - y) * rows, rows), rows)
-        mine = pl.ds(pl.multiple_of(y * rows, rows), rows)
-        s_y[c] = (keep0[slot, theirs] + r_core[c, theirs].astype(jnp.float32)).astype(jnp.bfloat16)
-        y_rs(c).start()
-        keep1[slot] = keep0[slot, mine] + r_core[c, mine].astype(jnp.float32)
-
-    def sum_y(c):
-        slot = lax.rem(c, 2)
-        y_rs(c).wait_recv()
-        s_z[c] = (keep1[slot] + r_y[c].astype(jnp.float32)).astype(jnp.bfloat16)
-        for o in z_others:
-            z_rs_to(c, o).start()
-        mine = pl.ds(pl.multiple_of(z * block, block), block)
-        keep2[slot] = keep1[slot, mine] + r_y[c, mine].astype(jnp.float32)
-
-    def sum_z(c):
-        slot = lax.rem(c, 2)
-        total = keep2[slot]
-        for o in z_others:
-            z_rs_from(c, o).wait_recv()
-            total = total + r_z[c, o].astype(jnp.float32)
-        pre = total * scale[z_rows(z), :][:, :1]
-        hidden = 0.5 * pre * (1.0 + lax.erf(pre * 0.7071067811865476))
-        gath[c, core, z_rows(z)] = hidden.astype(jnp.bfloat16)
-        for o in z_others:
-            z_ag_to(c, o).start()
-
-    def gather_z(c):
-        for o in z_others:
-            z_ag_from(c, o).wait_recv()
-        y_part(c, y).start()
-
-    def gather_y(c):
-        y_part(c, 1 - y).wait_recv()
+        keep[c] += r_core[c].astype(jnp.float32)
+
+    def spread_core(c):
         core_part(c, core).start()
 
     def down(c):
@@ -179,8 +284,34 @@
         def _():
             down_copy(c + 2, slot).start()
 
-    stages = [(5, gather_y), (4, gather_z), (3, sum_z), (2, sum_y), (1, sum_core), (0, up), (6, down)]
-
+    def both(*parts):
+        def run(zf, c):
+            for part in parts:
+                part(zf, c)
+
+        return run
+
+    def plain(part):
+        return lambda zf, c: part(c)
+
+    y_first = [
+        (13, both(gathered_y, plain(spread_core))),
+        (11, both(gathered_z, spread_y)),
+        (9, forward_z),
+        (7, both(take_z, activate, spread_z)),
+        (5, merge_z),
+        (3, both(take_y, send_z)),
+        (1, both(plain(sum_core), send_y)),
+    ]
+    z_first = [
+        (13, both(gathered_z, plain(spread_core))),
+        (11, forward_z),
+        (9, both(gathered_y, spread_z)),
+        (7, both(take_y, activate, spread_y)),
+        (5, both(take_z, send_y)),
+        (3, merge_z),
+        (1, both(plain(sum_core), send_z)),
+    ]
     def step(t, carry):
         @pl.when(t == 1)
         def _():
@@ -204,7 +335,16 @@
             row_scale = lax.rsqrt(total / (depth * n) + 1e-06)
             scale[...] = jnp.broadcast_to(row_scale[:1], (128, batch)).T
 
-        for offset, stage in stages:
+        for first, second in zip(y_first, z_first):
+            for zf, (offset, stage) in ((False, first), (True, second)):
+                c = t - offset
+                kind = (lax.rem(c, EVERY) == EVERY - 1) == zf
+
+                @pl.when(jnp.logical_and(jnp.logical_and(c >= 0, c < chunks), kind))
+                def _(c=c, stage=stage, zf=zf):
+                    stage(zf, c)
+
+        for offset, stage in ((0, up), (LAST, down)):
             c = t - offset
 
             @pl.when(jnp.logical_and(c >= 0, c < chunks))
@@ -213,7 +353,7 @@
 
         return carry
 
-    lax.fori_loop(0, chunks + 6, step, 0)
+    lax.fori_loop(0, chunks + LAST, step, 0)
 
     out[...] = acc[...].astype(jnp.bfloat16)
 
@@ -222,14 +362,38 @@
     for o in z_others:
         sq_to(o).wait_send()
 
+    def drain_kind(zf, c):
+        y_rs(zf, c).wait_send()
+        y_part(zf, c, y).wait_send()
+        if not tree:
+            for o in z_others:
+                z_direct(zf, c, o, z).wait_send()
+                g_direct(zf, c, o, z).wait_send()
+            return
+
+        @pl.when(at_end)
+        def _():
+            z_end(zf, c).wait_send()
+
+        @pl.when(in_middle)
+        def _():
+            z_mid(zf, c).wait_send()
+            z_merged(zf, c, 0).wait_send()
+            z_merged(zf, c, 1).wait_send()
+            g_two(zf, c).wait_send()
+
+        g_near(zf, c, z).wait_send()
+        g_far(zf, c, z, 1).wait_send()
+
     def drain(c, carry):
         core_rs(c).wait_send()
-        y_rs(c).wait_send()
-        for o in z_others:
-            z_rs_to(c, o).wait_send()
-            z_ag_to(c, o).wait_send()
-        y_part(c, y).wait_send()
         core_part(c, core).wait_send()
+        for zf in (False, True):
+
+            @pl.when((lax.rem(c, EVERY) == EVERY - 1) == zf)
+            def _(zf=zf):
+                drain_kind(zf, c)
+
         return carry
 
     lax.fori_loop(0, chunks, drain, 0)
@@ -240,7 +404,6 @@
     width = w_up.shape[1]
     chunks = width // CHUNK
     half, rows, nz = CHUNK // 2, batch // 2, n // 4
-    block = rows // nz
     bf16, f32 = jnp.bfloat16, jnp.float32
     vmem, dma = pltpu.VMEM, pltpu.SemaphoreType.DMA
     in_vmem = pl.BlockSpec(memory_space=pltpu.VMEM)
@@ -256,15 +419,15 @@
             vmem((batch, 128), f32),
             vmem((2, 2, depth, half), bf16),
             vmem((2, CHUNK, depth), bf16),
-            vmem((2, batch, half), f32),
-            vmem((2, rows, half), f32),
-            vmem((2, block, half), f32),
+            vmem((chunks, batch, half), f32),
             vmem((chunks, batch, half), bf16),
             vmem((chunks, batch, half), bf16),
             vmem((chunks, rows, half), bf16),
             vmem((chunks, rows, half), bf16),
-            vmem((chunks, rows, half), bf16),
-            vmem((chunks, nz, block, half), bf16),
+            vmem((chunks, batch, half), bf16),
+            vmem((chunks, batch, half), bf16),
+            vmem((chunks, 2, batch // nz, half), bf16),
+            vmem((chunks, 2, batch // nz, half), bf16),
             vmem((chunks, 2, batch, half), bf16),
             vmem((3, 8, batch), f32),
             vmem((2, 8, batch), f32),

time: 130 us -> 112 us (0.86)
  Pallas kernels: 126 us -> 108 us
    pallas_call x1, Pallas kernels: 126 us -> 108 us  [local(): pl.pallas_call(functools.partial(kernel, (n, depth, width, chunks)), out_...]
where the time goes in v2:
time: 112 us; the launch traced here: 111 us
  Pallas kernels  108 us (96%)
  local copies, waits for them, and re-layouts  3.67 us (3%)
    pallas_call x1, Pallas kernels, local(): pl.pallas_call(functools.partial(kernel, (n, depth, width, chunks)), out_...  108 us
    unnamed x1, local copies, waits for them, and re-layouts  2.37 us

profile of v2, /device:TPU:0, one launch (start us, length us, event | category | flops | bytes accessed | tf_op | source)
XLA Modules:
  0.0 111.3 jit_solution(14361372660368756733)
XLA Ops:
  0.0 1.3 %broadcast_in_dim.3.gain = f32[1,1152]{1,0:T(1,128)} reshape(f32[1152]{0:T(1024)} %param.5) | data formatting | bytes 9216 | tf_op jit(solution)/shard_map/broadcast_in_dim | solution.py:460
  1.3 107.6 %shard_map.46 = bf16[512,1152]{1,0:T(8,128)(2,1)} custom-call(bf16[512,1152]{1,0:T(8,128)(2,1)} %act.1, f32[1,1152]{1,0:T(1,128)} %broadcast_in_dim.3.gain, bf16[1152,8192]{1,0:T(8,128)(2,1)} %wup.1, bf16[8192,1152]{1,0:T(8,128)(2,1)} %wdn.1), custom_call_target="tpu_custom_call" | custom-call | flops 19327352832 | bytes 37748736 | tf_op jit(solution)/shard_map/pallas_call | solution.py:411
  108.9 2.4 %copy.6 = bf16[512,1152]{1,0:T(8,128)(2,1)} copy(bf16[512,1152]{1,0:T(8,128)(2,1)} %shard_map.46) | data formatting | bytes 2359296
